TPU v7x, 256 devices: a whole 4x4x8 slice. The times are simulated.
256 devices in a mesh: blk: 8 (over y_lo, x), rows: 32 (over y_hi, z, core).
Axes of the slice: x: 4, y: 4 (y_hi: 2, y_lo: 2; y = y_hi * 2 + y_lo), z: 8, core: 2. Of those that a mesh axis runs over, the one named last changes fastest.
Arguments:
- embeddings: bfloat16 [524288, 768], P(('blk', 'rows')), may hold values from -6 to 6
- coverage: float32 [524288], P(('blk', 'rows')), may hold values from 0 to 4
- chosen_index: int32 [512], replicated, may hold values from 0 to 524287, as said below
- candidate_index: int32 [1024], P('blk'), may hold values from 0 to 524287, as said below
Outputs:
- new_coverage: float32 [524288], P(('blk', 'rows'))
- gains: float32 [1024], P(('blk', 'rows'))
Inputs may be any that keep to these rules, and one draw needn't show every extreme that they name: `chosen_index`: the entries are distinct; the rows r * 2048 to (r + 1) * 2048 - 1 hold at most 4 of them for every r, and exactly 4 for some r. `candidate_index`: entries b * 128 to (b + 1) * 128 - 1 lie in rows b * 65536 to (b + 1) * 65536 - 1.
All inputs are finite; a program needn't handle non-finite values.
Results may differ from a plain program's by a relative error of at most 0.00035.
Values may be sent and summed in bfloat16 or wider, within the bound.
No kernel may reach another device: no remote copies, remote signals or barrier semaphores. Data moves between devices by JAX's collectives and lax.ppermute only.
A program may use at most 64 MiB of HBM per device.

v0:
```python
import jax
import jax.numpy as jnp
from jax import lax
from jax.sharding import Mesh
from jax.sharding import PartitionSpec as P

BLK = ("blk_0", "blk_1")
BLK_ROWS = ("blk_0", "blk_1", "rows")


def in_order(pieces, dim):
    pieces = jnp.moveaxis(pieces, 0, dim)
    dims = pieces.shape
    return pieces.reshape(*dims[:dim], dims[dim] * dims[dim + 1], *dims[dim + 2 :])


def all_blocks(x, axes, sequence):
    pieces = x[None]
    for k in sequence:
        pieces = lax.all_gather(pieces, axes[k], axis=0, tiled=True)
    held = [lax.axis_size(axes[k]) for k in reversed(sequence)]
    pieces = pieces.reshape(*held, *x.shape)
    turned = sorted(range(len(sequence)), key=lambda place: sequence[len(sequence) - 1 - place])
    return pieces.transpose(*turned, *range(len(sequence), pieces.ndim)).reshape(-1, *x.shape)


def whole_of(x, axes, sequence, dim):
    return in_order(all_blocks(x, axes, sequence), dim)


def owned_rows(embeddings, indices, base_row):
    local_rows = embeddings.shape[0]
    offset = indices - base_row
    inside = (offset >= 0) & (offset < local_rows)
    safe = jnp.clip(offset, 0, local_rows - 1)
    picked = jnp.take(embeddings, safe, axis=0).astype(jnp.float32)
    return jnp.where(inside[:, None], picked, 0.0)


def local(embeddings, coverage, chosen_index, candidate_index):
    local_rows = embeddings.shape[0]
    width = embeddings.shape[1]
    scale = 1.0 / width**0.5
    device_pos = lax.axis_index(BLK) * lax.axis_size("rows") + lax.axis_index("rows")
    base_row = device_pos * local_rows
    chosen_f = lax.psum(owned_rows(embeddings, chosen_index, base_row), BLK_ROWS)
    chosen_rows = chosen_f.astype(jnp.bfloat16)
    sims = jnp.dot(embeddings, chosen_rows.T, preferred_element_type=jnp.float32) * scale
    best = jnp.max(sims, axis=1)
    new_coverage = jnp.maximum(coverage, best)
    every_index = whole_of(candidate_index, BLK, (0, 1), 0)
    every_f = lax.psum(owned_rows(embeddings, every_index, base_row), BLK_ROWS)
    every_rows = every_f.astype(jnp.bfloat16)
    cand_sims = jnp.dot(embeddings, every_rows.T, preferred_element_type=jnp.float32) * scale
    gain_part = jnp.sum(jnp.maximum(cand_sims - new_coverage[:, None], 0.0), axis=0)
    gains = lax.psum_scatter(gain_part, BLK_ROWS, scatter_dimension=0, tiled=True)
    return (new_coverage, gains)


def solution(mesh):
    torus = Mesh(mesh.devices.reshape(2, 4, mesh.shape["rows"]), ("blk_0", "blk_1", "rows"))
    return jax.shard_map(
        local,
        mesh=torus,
        in_specs=(P(BLK_ROWS, None), P(BLK_ROWS), P(), P(BLK)),
        out_specs=(P(BLK_ROWS), P(BLK_ROWS)),
        check_vma=False,
    )
```

profile of v0, /device:TPU:1, one launch (start us, length us, event | category | flops | bytes accessed | tf_op | source)
XLA Modules:
  0.0 248.3 jit_solution(17189368050249611175)
XLA Ops:
  0.6 0.0 copy-start
  0.7 0.8 compare_and_fusion.1
  1.5 1.0 copy-done
  2.5 0.0 copy-start.4
  2.5 2.7 %gather_fusion = bf16[512,768]{1,0:T(8,128)(2,1)} fusion(bf16[2048,768]{1,0:T(8,128)(2,1)S(1)} %copy-done, s32[1024]{0:T(1024)S(1)} %pad_clamp_fusion), kind=kCustom, calls=%fused_computation | custom fusion | bytes 1574912 | tf_op jit(solution)/shard_map/jit(_take)/gather | solution.py:36
  5.2 2.5 %convert_select_fusion.1 = f32[512,768]{1,0:T(8,128)} fusion(bf16[512,768]{1,0:T(8,128)(2,1)} %gather_fusion, pred[512]{0:T(512)(128)(4,1)S(1)} %get-tuple-element.4, pred[512]{0:T(512)(128)(4,1)S(1)} %get-tuple-element.6), kind=kLoop, calls=%fused_computation.6 | loop fusion | flops 1179648 | bytes 2360320 | tf_op jit(solution)/shard_map/jit(_where)/select_n | solution.py:37
  7.8 0.0 copy-done.4
  7.8 3.7 %all-gather.1 = s32[2,1,128]{2,1,0:T(1,128)S(1)} all-gather(s32[1,1,128]{2,1,0:T(1,128)S(1)} %bitcast.19), channel_id=2, replica_groups=mesh['blk_0'=2,'blk_1'=4,'rows'=32] {'blk_0'}, dimensions={0}, use_global_device_ids=true | all-gather | bytes 1536 | tf_op jit(solution)/shard_map/all_gather | solution.py:20
  11.5 7.9 %all-gather.2 = s32[4,2,128]{2,1,0:T(2,128)S(1)} all-gather(s32[1,2,128]{2,1,0:T(2,128)S(1)} %bitcast.18), channel_id=1, replica_groups=mesh['blk_0'=2,'blk_1'=4,'rows'=32] {'blk_1'}, dimensions={0}, use_global_device_ids=true | all-gather | bytes 5120 | tf_op jit(solution)/shard_map/all_gather | solution.py:20
  19.4 5.2 %gather_fusion.1 = bf16[1024,768]{1,0:T(8,128)(2,1)} fusion(bf16[2048,768]{1,0:T(8,128)(2,1)S(1)} %copy-done, s32[1024]{0:T(1024)S(1)} %broadcast_clamp_fusion), kind=kCustom, calls=%fused_computation.1 | custom fusion | bytes 3149824 | tf_op jit(solution)/shard_map/jit(_take)/gather | solution.py:36
  24.7 3.2 %convert_select_fusion = f32[1024,768]{1,0:T(8,128)} fusion(bf16[1024,768]{1,0:T(8,128)(2,1)} %gather_fusion.1, pred[1024]{0:T(1024)(128)(4,1)S(1)} %compare_and_fusion, pred[1024]{0:T(1024)(128)(4,1)S(1)} %bitcast.17), kind=kLoop, calls=%fused_computation.4 | loop fusion | flops 2359296 | bytes 4720640 | tf_op jit(solution)/shard_map/jit(_where)/select_n | solution.py:37
  27.9 138.1 %all-reduce.3 = (bf16[512,768]{1,0:T(8,128)(2,1)}, bf16[1024,768]{1,0:T(8,128)(2,1)}) all-reduce(f32[512,768]{1,0:T(8,128)} %convert_select_fusion.1, f32[1024,768]{1,0:T(8,128)} %convert_select_fusion), channel_id=1, replica_groups=mesh['blk_0'=2,'blk_1'=4,'rows'=32] {'blk_0','blk_1','rows'}, use_global_device_ids=true, to_apply=%region_0.1 | all-reduce | flops 1179648 | bytes 7077888 | tf_op jit(solution)/shard_map/psum | solution.py:46
  166.0 0.0 copy-start.1
  166.0 0.0 copy-start.3
  166.0 3.1 %multiply_reduce_fusion = f32[2048]{0:T(1024)S(1)} fusion(bf16[2048,768]{1,0:T(8,128)(2,1)S(1)} %copy-done, bf16[512,768]{1,0:T(8,128)(2,1)} %get-tuple-element.2), kind=kOutput, calls=%fused_computation.3 | convolution fusion | flops 1612707840 | bytes 3940352 | tf_op jit(solution)/shard_map/dot_general | solution.py:48
  169.1 0.0 copy-done.1
  169.1 0.0 copy-start.2
  169.2 0.0 copy-done.3
  169.2 3.9 %maximum_reduce_fusion = f32[1024]{0:T(1024)S(1)} fusion(bf16[2048,768]{1,0:T(8,128)(2,1)S(1)} %copy-done, f32[2048]{0:T(1024)S(1)} %max.18, bf16[1024,768]{1,0:T(8,128)(2,1)S(1)} %copy-done.3), kind=kOutput, calls=%fused_computation.2 | convolution fusion | flops 3229613056 | bytes 4730880 | tf_op jit(solution)/shard_map/dot_general | solution.py:54
  173.0 0.0 copy-done.2
  173.0 74.7 %all-reduce = f32[1024]{0:T(1024)S(1)} all-reduce(f32[1024]{0:T(1024)S(1)} %maximum_reduce_fusion), channel_id=3, replica_groups=mesh['blk_0'=2,'blk_1'=4,'rows'=32] {'blk_0','blk_1','rows'}, use_global_device_ids=true, to_apply=%region_4.5.clone | all-reduce | flops 1024 | bytes 8192
  247.8 0.6 dynamic-slice
  (9 shorter events, 0.1 us)
Async XLA Ops:
  0.6 1.9 copy-start
  2.5 5.3 %copy-start.4 = (s32[128]{0:T(128)S(1)}, s32[128]{0:T(128)}, u32[]{:S(2)}) copy-start(s32[128]{0:T(128)} %param.7) | copy-start | bytes 1540
  166.0 3.1 %copy-start.1 = (f32[2048]{0:T(1024)S(1)}, f32[2048]{0:T(1024)}, u32[]{:S(2)}) copy-start(f32[2048]{0:T(1024)} %param.5) | copy-start | bytes 24580
  166.0 3.1 %copy-start.3 = (bf16[1024,768]{1,0:T(8,128)(2,1)S(1)}, bf16[1024,768]{1,0:T(8,128)(2,1)}, u32[]{:S(2)}) copy-start(bf16[1024,768]{1,0:T(8,128)(2,1)} %get-tuple-element.3) | copy-start | bytes 4718596
  169.1 3.9 %copy-start.2 = (f32[2048]{0:T(1024)}, f32[2048]{0:T(1024)S(1)}, u32[]{:S(2)}) copy-start(f32[2048]{0:T(1024)S(1)} %max.18) | copy-start | bytes 24580
where the time goes:
time: 249 us; the launch traced here: 248 us
  blocking collectives  224 us (90%)
  local copies, waits for them, and re-layouts  9.6 us (4%)
  matrix products  6.95 us (3%)
  other arithmetic  6.67 us (3%)
    psum x1, blocking collectives, local(): lax.psum(owned_rows(embeddings, chosen_index, base_row), BLK_ROWS)  138 us
    unnamed x1, blocking collectives  74.7 us
    all_gather x2, blocking collectives, all_blocks(): pieces = lax.all_gather(pieces, axes[k], axis=0, tiled=True)  11.6 us
    gather x2, local copies, waits for them, and re-layouts, owned_rows(): picked = jnp.take(embeddings, safe, axis=0).astype(jnp.float32)  7.95 us
    select_n x2, other arithmetic, owned_rows(): return jnp.where(inside[:, None], picked, 0.0)  5.78 us

commit v1 on v0

--- a/solution.py
+++ b/solution.py
@@ -43,7 +43,9 @@
     scale = 1.0 / width**0.5
     device_pos = lax.axis_index(BLK) * lax.axis_size("rows") + lax.axis_index("rows")
     base_row = device_pos * local_rows
-    chosen_f = lax.psum(owned_rows(embeddings, chosen_index, base_row), BLK_ROWS)
+    chosen_f = lax.psum(
+        lax.psum(owned_rows(embeddings, chosen_index, base_row), "blk_0"), ("blk_1", "rows")
+    )
     chosen_rows = chosen_f.astype(jnp.bfloat16)
     sims = jnp.dot(embeddings, chosen_rows.T, preferred_element_type=jnp.float32) * scale
     best = jnp.max(sims, axis=1)

time: 249 us -> 916 us (3.68)
  blocking collectives: 224 us -> 878 us
  between operations: 0.73 us -> 14.1 us
    psum x1 -> x2, blocking collectives: 138 us -> 788 us  [the longest x1 654 us: local(): lax.psum(lax.psum(owned_rows(embeddings, chosen_index, base_row), 'blk_0'...]
  transfers between devices with their start and end apart: 0 -> 1, of which waited for: 0 -> 0; matrix products, arithmetic and copies ran while one was open for 0% -> 1% of each run, Pallas kernels for 0% -> 0%
where the time goes in v1:
time: 916 us; the launch traced here: 915 us
  blocking collectives  878 us (96%)
  between operations  14.1 us (2%)
  local copies, waits for them, and re-layouts  9.54 us (1%)
    psum x1, blocking collectives, local(): lax.psum(lax.psum(owned_rows(embeddings, chosen_index, base_row), 'blk_0'...  654 us
    psum x1, blocking collectives, local(): every_f = lax.psum(owned_rows(embeddings, every_index, base_row), BLK_ROWS)  134 us
    unnamed x1, blocking collectives  78.6 us
  transfers between devices with their start and end apart: 1, of which 0 were waited for; matrix products, arithmetic and copies ran while one was open for 1% of the time, Pallas kernels for 0%

profile of v1, /device:TPU:1, one launch (start us, length us, event | category | flops | bytes accessed | tf_op | source)
XLA Modules:
  0.0 915.3 jit_solution(15018406382673319933)
XLA Ops:
  7.2 0.0 copy-start
  7.2 0.0 all-reduce.5.cloned.1.call-start
  7.2 0.8 compare_and_fusion.1
  8.1 1.0 copy-done
  9.1 2.7 gather_fusion
  11.8 0.0 copy-start.4
  11.8 2.6 convert_select_fusion.1
  14.4 0.0 all-reduce.5.cloned.1.call-update
  14.4 0.0 copy-done.4
  14.4 3.7 all-gather.1
  18.1 7.9 all-gather.2
  26.1 5.2 gather_fusion.1
  31.3 3.2 convert_select_fusion
  34.5 134.1 %all-reduce.7 = bf16[1024,768]{1,0:T(8,128)(2,1)} all-reduce(f32[1024,768]{1,0:T(8,128)} %convert_select_fusion), channel_id=1, replica_groups=mesh['blk_0'=2,'blk_1'=4,'rows'=32] {'blk_0','blk_1','rows'}, use_global_device_ids=true, to_apply=%region_3.4 | all-reduce | flops 786432 | bytes 4718592 | tf_op jit(solution)/shard_map/psum | solution.py:54
  168.6 0.0 all-reduce.5.cloned.1.call-done
  168.6 653.7 %all-reduce.6 = bf16[512,768]{1,0:T(8,128)(2,1)} all-reduce(f32[512,768]{1,0:T(8,128)} %all-reduce.5.cloned.1.call-done), channel_id=1, replica_groups=mesh['blk_0'=2,'blk_1'=4,'rows'=32] {'blk_1','rows'}, use_global_device_ids=true, to_apply=%region_1.2 | all-reduce | flops 393216 | bytes 2359296 | tf_op jit(solution)/shard_map/psum | solution.py:46
  822.3 0.0 copy-start.2
  822.3 0.0 copy-start.1
  822.3 3.1 multiply_reduce_fusion
  825.4 0.0 copy-done.2
  825.4 0.0 copy-done.1
  825.4 0.0 copy-start.3
  825.4 3.9 maximum_reduce_fusion
  829.3 0.0 copy-done.3
  829.3 78.6 %all-reduce = f32[1024]{0:T(1024)S(1)} all-reduce(f32[1024]{0:T(1024)S(1)} %maximum_reduce_fusion), channel_id=3, replica_groups=mesh['blk_0'=2,'blk_1'=4,'rows'=32] {'blk_0','blk_1','rows'}, use_global_device_ids=true, to_apply=%region_5.6.clone | all-reduce | flops 1024 | bytes 8192
  907.9 0.6 dynamic-slice
  (9 shorter events, 0.1 us)
Async XLA Ops:
  7.2 1.9 copy-start
  7.2 161.5 %all-reduce.5.cloned.1.call-start = ((), (), s32[]{:S(2)}) async-start(), calls=%async_computation | async-start | bytes 3145728 | tf_op jit(solution)/shard_map/psum | solution.py:47
  11.8 2.6 copy-start.4
  822.3 3.1 copy-start.2
  822.3 3.1 copy-start.1
  825.4 3.9 copy-start.3
Sparse Core Ops, SparseCore 0:
  14.5 72.0 all-reduce.4
